TPU v7x, 32 devices: a whole 2x2x4 slice. The times are simulated.
32 devices in a mesh: groups: 2 (over x), attn: 2 (over core), expert: 8 (over z, y).
Axes of the slice: x: 2, y: 2, z: 4, core: 2. Of those that a mesh axis runs over, the one named last changes fastest.
Arguments:
- hidden_a: bfloat16 [1024, 1440], P(('groups', 'attn', 'expert')), parts along dimension 0, may hold values from -6 to 6
- routes: int32 [1024, 4], P(('groups', 'attn', 'expert')), parts along dimension 0, may hold values from 0 to 15, all different within a row; in each aligned block of 32 rows (0 to 31, 32 to 63, ...) at most 16 rows name the same one
- gate_w: bfloat16 [1024, 4], P(('groups', 'attn', 'expert')), parts along dimension 0, may hold values from 0.049804688 to 0.59765625
- w_gate: bfloat16 [16, 1440, 1440], P(('attn', 'expert')), may hold values from -0.15625 to 0.15625
- w_up: bfloat16 [16, 1440, 1440], P(('attn', 'expert')), may hold values from -0.15625 to 0.15625
- w_down: bfloat16 [16, 1440, 1440], P(('attn', 'expert')), may hold values from -0.15625 to 0.15625
Outputs:
- mixed: bfloat16 [1024, 1440], P(('groups', 'attn', 'expert')), parts along dimension 0
There are 2 independent parts, one for each index of `groups`. A program takes and returns all parts, laid end to end along the dimension named above; an argument that names none is the same for every part. Nothing has to cross between parts.
Inputs may be any that keep to these rules, and one draw needn't show every extreme that they name: `routes`: in the rows of one device, each expert is named by at most 16 rows; a token names 4 different experts.
All inputs are finite; a program needn't handle non-finite values.
Results may differ from a plain program's by a relative error of at most 0.0058.
Values may be sent and summed in bfloat16 or wider, within the bound.
A program may use at most 64 MiB of HBM per device.

v0:
```python
import jax
import jax.numpy as jnp
from jax import lax
from jax.sharding import PartitionSpec as P


def body(hidden_a, routes, gate_w, w_gate, w_up, w_down):
    experts = lax.axis_size(("attn", "expert"))
    tok_dev, top_k = routes.shape
    width = hidden_a.shape[1]
    capacity = 2 * tok_dev * top_k // experts
    flat = routes.reshape(-1)
    hits = (flat[:, None] == jnp.arange(experts, dtype=jnp.int32)[None, :]).astype(jnp.int32)
    rank = jnp.sum((jnp.cumsum(hits, axis=0) - hits) * hits, axis=1)
    position = flat * capacity + rank
    source = (
        jnp.full((experts * capacity,), -1, dtype=jnp.int32)
        .at[position]
        .set(jnp.arange(tok_dev * top_k, dtype=jnp.int32))
    )
    live = source >= 0
    safe = jnp.maximum(source, 0)
    send_rows = jnp.where(live[:, None], hidden_a[safe // top_k], jnp.zeros((), jnp.bfloat16))
    send_rows = send_rows.reshape(experts, capacity, width)
    send_weights = jnp.where(live, gate_w.reshape(-1)[safe], jnp.zeros((), jnp.bfloat16))
    send_weights = send_weights.reshape(experts, capacity)
    gate_matrix = w_gate[0]
    up_matrix = w_up[0]
    down_matrix = w_down[0]
    weights = lax.all_to_all(
        send_weights, ("attn", "expert"), split_axis=0, concat_axis=0, tiled=True
    )
    senders, slots = weights.shape
    flat_rows = lax.all_to_all(
        send_rows, ("attn", "expert"), split_axis=0, concat_axis=0, tiled=True
    ).reshape(senders * slots, width)
    gate = jnp.dot(flat_rows, gate_matrix, preferred_element_type=jnp.float32)
    up = jnp.dot(flat_rows, up_matrix, preferred_element_type=jnp.float32)
    hidden = (jax.nn.silu(gate) * up).astype(jnp.bfloat16)
    down = jnp.dot(hidden, down_matrix, preferred_element_type=jnp.float32)
    scaled = weights.reshape(-1, 1).astype(jnp.float32) * down
    produced = scaled.astype(jnp.bfloat16).reshape(senders, slots, width)
    returned = lax.all_to_all(produced, ("attn", "expert"), split_axis=0, concat_axis=0, tiled=True)
    results = returned.reshape(experts * capacity, width)
    taken = results[position]
    mixed = jnp.sum(taken.astype(jnp.float32).reshape(tok_dev, top_k, width), axis=1).astype(
        jnp.bfloat16
    )
    return mixed


def solution(mesh):
    placed = (
        P(("groups", "attn", "expert"), None),
        P(("groups", "attn", "expert"), None),
        P(("groups", "attn", "expert"), None),
        P(("attn", "expert"), None, None),
        P(("attn", "expert"), None, None),
        P(("attn", "expert"), None, None),
    )
    return jax.shard_map(
        body,
        mesh=mesh,
        in_specs=placed,
        out_specs=P(("groups", "attn", "expert"), None),
        check_vma=False,
    )
```

profile of v0, /device:TPU:0, one launch (start us, length us, event | category | flops | bytes accessed | tf_op | source)
XLA Modules:
  0.0 85.7 jit_solution(9787221805058316996)
XLA Ops:
  0.0 0.0 copy-start
  0.0 0.8 copy.16
  0.8 0.7 broadcast_multiply_fusion
  1.5 0.1 eq.15
  1.6 0.1 fusion.21
  1.7 0.2 reduce_window_sum.11
  1.9 0.2 select_reduce_fusion
  2.0 0.1 copy.15
  2.1 0.1 mul.36
  2.3 1.0 %scatter_custom_fusion = s32[256]{0:T(256)S(1)} fusion(s32[128]{0:T(128)S(1)} %fusion.22, s32[128]{0:T(128)S(1)} %iota.7, s32[]{:T(128)} %constant.31.clone.1), kind=kCustom, calls=%fused_computation.31 | custom fusion | bytes 1028 | tf_op jit(solution)/shard_map/scatter | solution.py:19
  3.3 0.8 copy.17
  4.0 0.1 reshape.67
  4.2 1.9 %gather_fusion = bf16[256]{0:T(256)(128)(2,1)S(1)} fusion(bf16[128]{0:T(256)(128)(2,1)S(1)} %reshape.67, s32[1024]{0:T(1024)S(1)} %get-tuple-element.10), kind=kCustom, calls=%fused_computation | custom fusion | bytes 2048 | tf_op jit(solution)/shard_map/gather | solution.py:25
  6.1 0.7 all_to_all.16
  6.7 7.4 %all-to-all-start = ((bf16[16,1,16]{2,1,0:T(2,128)(2,1)}), bf16[16,1,16]{2,1,0:T(2,128)(2,1)S(1)}, u32[]{:S(2)}, u32[]{:S(2)}) async-start(bf16[16,1,16]{2,1,0:T(2,128)(2,1)} %all_to_all.16), calls=%async_computation | async-start | bytes 16384 | tf_op jit(solution)/shard_map/all_to_all | solution.py:30
  14.1 0.1 broadcast_in_dim.34
  14.2 0.0 copy-done
  14.2 1.3 %gather_fusion.1 = bf16[256,1440]{1,0:T(8,128)(2,1)S(1)} fusion(bf16[32,1440]{1,0:T(8,128)(2,1)S(1)} %copy-done, s32[1024]{0:T(1024)S(1)} %get-tuple-element.9), kind=kCustom, calls=%fused_computation.1 | custom fusion | bytes 1475584 | tf_op jit(solution)/shard_map/gather | solution.py:23
  15.5 1.0 %broadcast_select_fusion = bf16[16,16,1440]{2,1,0:T(8,128)(2,1)} fusion(bf16[16,16,1440]{2,1,0:T(8,128)(2,1)S(1)} %bitcast.32, pred[16,16]{1,0:T(8,128)(4,1)S(1)} %broadcast_in_dim.34), kind=kLoop, calls=%fused_computation.14 | loop fusion | flops 368640 | bytes 1474816 | tf_op jit(solution)/shard_map/jit(_where)/select_n | solution.py:23
  16.5 4.0 %all-to-all-done = bf16[16,1,16]{2,1,0:T(2,128)(2,1)S(1)} async-done(((bf16[16,1,16]{2,1,0:T(2,128)(2,1)}), bf16[16,1,16]{2,1,0:T(2,128)(2,1)S(1)}, u32[]{:S(2)}, u32[]{:S(2)}) %all-to-all-start) | async-done | bytes 544 | tf_op jit(solution)/shard_map/all_to_all | solution.py:30
  20.5 3.6 %all-to-all-start.1 = ((bf16[16,16,1440]{2,1,0:T(8,128)(2,1)}), bf16[16,16,1440]{2,1,0:T(8,128)(2,1)S(1)}, u32[]{:S(2)}, u32[]{:S(2)}) async-start(bf16[16,16,1440]{2,1,0:T(8,128)(2,1)} %broadcast_select_fusion), calls=%async_computation.1 | async-start | bytes 1572864 | tf_op jit(solution)/shard_map/all_to_all | solution.py:34
  24.1 0.1 reshape.71
  24.2 21.0 %all-to-all-done.1 = bf16[16,16,1440]{2,1,0:T(8,128)(2,1)S(1)} async-done(((bf16[16,16,1440]{2,1,0:T(8,128)(2,1)}), bf16[16,16,1440]{2,1,0:T(8,128)(2,1)S(1)}, u32[]{:S(2)}, u32[]{:S(2)}) %all-to-all-start.1) | async-done | bytes 737312 | tf_op jit(solution)/shard_map/all_to_all | solution.py:34
  45.2 4.2 %fusion.4 = f32[256,1440]{0,1:T(8,128)S(1)} fusion(bf16[256,1440]{1,0:T(8,128)(2,1)S(1)} %bitcast.33, bf16[1,1440,1440]{2,1,0:T(8,128)(2,1)} %param.9), kind=kOutput, calls=%fused_computation.8 | convolution fusion | flops 1061683200 | bytes 6359040 | tf_op jit(solution)/shard_map/dot_general | solution.py:37
  49.3 8.3 %fusion.12 = bf16[256,1440]{0,1:T(8,128)(2,1)S(1)} fusion(bf16[1,1440,1440]{2,1,0:T(8,128)(2,1)} %param.11, bf16[256,1440]{1,0:T(8,128)(2,1)S(1)} %bitcast.34, bf16[1,1440,1440]{2,1,0:T(8,128)(2,1)} %param.10, f32[256,1440]{0,1:T(8,128)S(1)} %fusion.4, f32[256]{0:T(256)S(1)} %reshape.71), kind=kOutput, calls=%fused_computation.12 | convolution fusion | flops 2126315520 | bytes 11244544 | tf_op jit(solution)/shard_map/dot_general | solution.py:40
  57.7 1.2 %copy.19 = bf16[256,1440]{1,0:T(8,128)(2,1)} copy(bf16[256,1440]{0,1:T(8,128)(2,1)S(1)} %fusion.12) | data formatting | bytes 1474560 | tf_op jit(solution)/shard_map/convert_element_type | solution.py:42
  58.8 3.6 %all-to-all-start.2 = ((bf16[16,16,1440]{2,1,0:T(8,128)(2,1)}), bf16[16,16,1440]{2,1,0:T(8,128)(2,1)S(1)}, u32[]{:S(2)}, u32[]{:S(2)}) async-start(bf16[16,16,1440]{2,1,0:T(8,128)(2,1)} %bitcast.7), calls=%async_computation.2 | async-start | bytes 1572864 | tf_op jit(solution)/shard_map/all_to_all | solution.py:43
  62.4 21.1 %all-to-all-done.2 = bf16[16,16,1440]{2,1,0:T(8,128)(2,1)S(1)} async-done(((bf16[16,16,1440]{2,1,0:T(8,128)(2,1)}), bf16[16,16,1440]{2,1,0:T(8,128)(2,1)S(1)}, u32[]{:S(2)}, u32[]{:S(2)}) %all-to-all-start.2) | async-done | bytes 737312 | tf_op jit(solution)/shard_map/all_to_all | solution.py:43
  83.5 0.9 %gather_fusion.2 = bf16[128,1440]{1,0:T(8,128)(2,1)S(1)} fusion(bf16[256,1440]{1,0:T(8,128)(2,1)S(1)} %bitcast.31, s32[1024]{0:T(1024)S(1)} %pad_clamp_fusion), kind=kCustom, calls=%fused_computation.2 | custom fusion | bytes 737792 | tf_op jit(solution)/shard_map/gather | solution.py:45
  84.4 0.1 gather.17
  84.5 1.2 %reduce_sum.25 = bf16[32,1440]{1,0:T(8,128)(2,1)} reduce(bf16[32,4,1440]{2,1,0:T(4,128)(2,1)S(1)} %gather.17, bf16[]{:T(256)} %constant.35.clone.1), dimensions={1}, to_apply=%region_3.4 | reduce | flops 138240 | bytes 460802 | tf_op jit(solution)/shard_map/reduce_sum | solution.py:46
  (7 shorter events, 0.1 us)
Async XLA Ops:
  0.0 14.2 %copy-start = (bf16[32,1440]{1,0:T(8,128)(2,1)S(1)}, bf16[32,1440]{1,0:T(8,128)(2,1)}, u32[]{:S(2)}) copy-start(bf16[32,1440]{1,0:T(8,128)(2,1)} %param.6) | copy-start | bytes 276484
  6.7 13.7 %all-to-all-start = ((bf16[16,1,16]{2,1,0:T(2,128)(2,1)}), bf16[16,1,16]{2,1,0:T(2,128)(2,1)S(1)}, u32[]{:S(2)}, u32[]{:S(2)}) async-start(bf16[16,1,16]{2,1,0:T(2,128)(2,1)} %all_to_all.16), calls=%async_computation | async-start | bytes 16384 | tf_op jit(solution)/shard_map/all_to_all | solution.py:30
  20.5 24.7 %all-to-all-start.1 = ((bf16[16,16,1440]{2,1,0:T(8,128)(2,1)}), bf16[16,16,1440]{2,1,0:T(8,128)(2,1)S(1)}, u32[]{:S(2)}, u32[]{:S(2)}) async-start(bf16[16,16,1440]{2,1,0:T(8,128)(2,1)} %broadcast_select_fusion), calls=%async_computation.1 | async-start | bytes 1572864 | tf_op jit(solution)/shard_map/all_to_all | solution.py:34
  58.8 24.7 %all-to-all-start.2 = ((bf16[16,16,1440]{2,1,0:T(8,128)(2,1)}), bf16[16,16,1440]{2,1,0:T(8,128)(2,1)S(1)}, u32[]{:S(2)}, u32[]{:S(2)}) async-start(bf16[16,16,1440]{2,1,0:T(8,128)(2,1)} %bitcast.7), calls=%async_computation.2 | async-start | bytes 1572864 | tf_op jit(solution)/shard_map/all_to_all | solution.py:43
where the time goes:
time: 86.1 us; the launch traced here: 85.7 us
  waiting for transfers between devices  46 us (53%)
  starting transfers between devices  14.6 us (17%)
  matrix products  12.5 us (15%)
  local copies, waits for them, and re-layouts  9.11 us (11%)
  other arithmetic  3.35 us (4%)
    all_to_all x1, waiting for transfers between devices, body(): lax.all_to_all(produced, ('attn', 'expert'), split_axis=0, concat_axis=0,...  21.1 us
    all_to_all x1, waiting for transfers between devices, body(): lax.all_to_all(send_rows, ('attn', 'expert'), split_axis=0, concat_axis=0...  21 us
    dot_general x1, matrix products, body(): down = jnp.dot(hidden, down_matrix, preferred_element_type=jnp.float32)  8.31 us
    all_to_all x1, starting transfers between devices, body(): lax.all_to_all(send_weights, ('attn', 'expert'), split_axis=0, concat_axi...  7.39 us
    dot_general x1, matrix products, body(): gate = jnp.dot(flat_rows, gate_matrix, preferred_element_type=jnp.float32)  4.16 us
    all_to_all x1, waiting for transfers between devices, body(): lax.all_to_all(send_weights, ('attn', 'expert'), split_axis=0, concat_axi...  3.95 us
    all_to_all x1, starting transfers between devices, body(): lax.all_to_all(send_rows, ('attn', 'expert'), split_axis=0, concat_axis=0...  3.61 us
    all_to_all x1, starting transfers between devices, body(): lax.all_to_all(produced, ('attn', 'expert'), split_axis=0, concat_axis=0,...  3.61 us
  transfers between devices with their start and end apart: 3, of which 3 were waited for; matrix products, arithmetic and copies ran while one was open for 3% of the time, Pallas kernels for 0%

commit v1 on v0

v1 whole, which is shorter than its diff:
```python
import functools
import jax
import jax.numpy as jnp
from jax import lax
from jax.experimental import pallas as pl
from jax.experimental.pallas import tpu as pltpu
from jax.sharding import PartitionSpec as P

MESH = pl.DeviceIdType.MESH
FAR = 4
LANES = 128


def exchange_body(hidden_a, routes, gate_w, w_gate, w_up, w_down):
    experts = lax.axis_size(("attn", "expert"))
    tok_dev, top_k = routes.shape
    width = hidden_a.shape[1]
    capacity = 2 * tok_dev * top_k // experts
    flat = routes.reshape(-1)
    hits = (flat[:, None] == jnp.arange(experts, dtype=jnp.int32)[None, :]).astype(jnp.int32)
    rank = jnp.sum((jnp.cumsum(hits, axis=0) - hits) * hits, axis=1)
    position = flat * capacity + rank
    source = (
        jnp.full((experts * capacity,), -1, dtype=jnp.int32)
        .at[position]
        .set(jnp.arange(tok_dev * top_k, dtype=jnp.int32))
    )
    live = source >= 0
    safe = jnp.maximum(source, 0)
    send_rows = jnp.where(live[:, None], hidden_a[safe // top_k], jnp.zeros((), jnp.bfloat16))
    send_rows = send_rows.reshape(experts, capacity, width)
    send_weights = jnp.where(live, gate_w.reshape(-1)[safe], jnp.zeros((), jnp.bfloat16))
    send_weights = send_weights.reshape(experts, capacity)
    weights = lax.all_to_all(
        send_weights, ("attn", "expert"), split_axis=0, concat_axis=0, tiled=True
    )
    senders, slots = weights.shape
    flat_rows = lax.all_to_all(
        send_rows, ("attn", "expert"), split_axis=0, concat_axis=0, tiled=True
    ).reshape(senders * slots, width)
    gate = jnp.dot(flat_rows, w_gate[0], preferred_element_type=jnp.float32)
    up = jnp.dot(flat_rows, w_up[0], preferred_element_type=jnp.float32)
    hidden = (jax.nn.silu(gate) * up).astype(jnp.bfloat16)
    down = jnp.dot(hidden, w_down[0], preferred_element_type=jnp.float32)
    scaled = weights.reshape(-1, 1).astype(jnp.float32) * down
    produced = scaled.astype(jnp.bfloat16).reshape(senders, slots, width)
    returned = lax.all_to_all(produced, ("attn", "expert"), split_axis=0, concat_axis=0, tiled=True)
    results = returned.reshape(experts * capacity, width)
    taken = results[position]
    return jnp.sum(taken.astype(jnp.float32).reshape(tok_dev, top_k, width), axis=1).astype(
        jnp.bfloat16
    )


def tiles_of(total, step):
    return [(at, min(step, total - at)) for at in range(0, total, step)]


def kernel(
    hidden_ref, routes_ref, gates_ref, wg_hbm, wu_hbm, wd_hbm, out_ref,
    wg, wu, wd, x, h, y, from_core, to_y, from_y, to_z, from_z,
    load_sem, ag_send, ag_recv, core_send, core_recv, y_send, y_recv, z_send, z_recv,
):
    rows, top = routes_ref.shape
    width = hidden_ref.shape[1]
    ff = wg_hbm.shape[2]
    quad = FAR * rows

    group = lax.axis_index("groups")
    core = lax.axis_index("attn")
    place = lax.axis_index("expert")
    far, near = place // 2, place % 2
    own = core * lax.axis_size("expert") + place

    fars = [far, far + 1 - 2 * (far % 2), (far + 2) % FAR, FAR - 1 - far]
    sibling = (group, 1 - core, place)
    beside = (group, core, far * 2 + 1 - near)
    along = [(group, core, f * 2 + near) for f in fars]

    loads = [
        pltpu.make_async_copy(src.at[0], dst, load_sem.at[i])
        for i, (src, dst) in enumerate(((wg_hbm, wg), (wu_hbm, wu), (wd_hbm, wd)))
    ]
    for load in loads:
        load.start()

    barrier = pltpu.get_barrier_semaphore()
    partners = [sibling, beside] + along[1:]
    for partner in partners:
        pl.semaphore_signal(barrier, inc=1, device_id=partner, device_id_type=MESH)

    start = width // LANES * LANES
    rest = width - start
    x[0:rows, 0:start] = hidden_ref[:, 0:start]
    lane = lax.broadcasted_iota(jnp.int32, (rows, LANES), 1)
    table = jnp.zeros((rows, LANES), jnp.float32)
    for k in range(top):
        table += jnp.where(
            lane == routes_ref[:, k : k + 1] + rest, gates_ref[:, k : k + 1].astype(jnp.float32), 0.0
        )
    last = jnp.concatenate(
        [hidden_ref[:, start:].astype(jnp.float32), jnp.zeros((rows, LANES - rest), jnp.float32)], axis=1
    )
    x[0:rows, start : start + LANES] = (table + last).astype(jnp.bfloat16)
    pl.semaphore_wait(barrier, len(partners))

    def slot(dy, dc, d):
        return x.at[pl.ds(((dy * 2 + dc) * FAR + d) * rows, rows)]

    def remote(src, dst, send, recv, i, device):
        return pltpu.make_async_remote_copy(
            src_ref=src, dst_ref=dst, send_sem=send.at[i], recv_sem=recv.at[i],
            device_id=device, device_id_type=MESH,
        )

    gather_z = {d: remote(slot(0, 0, 0), slot(0, 0, d), ag_send, ag_recv, d - 1, along[d]) for d in (1, 2, 3)}
    gather_y = {d: remote(slot(0, 0, d), slot(1, 0, d), ag_send, ag_recv, 3 + d, beside) for d in range(FAR)}
    gather_c = {
        (dy, d): remote(slot(dy, 0, d), slot(dy, 1, d), ag_send, ag_recv, 7 + dy * FAR + d, sibling)
        for dy in range(2) for d in range(FAR)
    }
    for d in (3, 2, 1):
        gather_z[d].start()
    gather_y[0].start()
    gather_c[0, 0].start()
    for d in (1, 2, 3):
        gather_z[d].wait_recv()
        gather_y[d].start()
        gather_c[0, d].start()

    n_ff = tiles_of(ff, 512)
    n_out = tiles_of(width, 512)
    scale = {}

    def up_tile(dy, at, size):
        block = x[dy * 2 * quad : (dy + 1) * 2 * quad, 0:width]
        gate = jnp.dot(block, wg[:, at : at + size], preferred_element_type=jnp.float32)
        up = jnp.dot(block, wu[:, at : at + size], preferred_element_type=jnp.float32)
        h[:, at : at + size] = (gate / (1.0 + jnp.exp(-gate)) * up).astype(jnp.bfloat16)

    def down_tile(dy, at, size):
        if dy not in scale:
            tail = x[dy * 2 * quad : (dy + 1) * 2 * quad, start : start + LANES].astype(jnp.float32)
            lanes = lax.broadcasted_iota(jnp.int32, tail.shape, 1)
            scale[dy] = jnp.sum(jnp.where(lanes == own + rest, tail, 0.0), axis=1, keepdims=True)
        down = jnp.dot(h[...], wd[:, at : at + size], preferred_element_type=jnp.float32)
        y[dy * 2 * quad : (dy + 1) * 2 * quad, at : at + size] = (scale[dy] * down).astype(jnp.bfloat16)

    def core_copy(dy, j):
        at, size = n_out[j]
        columns = pl.ds(at, size)
        return remote(
            y.at[pl.ds((dy * 2 + 1) * quad, quad), columns],
            from_core.at[pl.ds(dy * quad, quad), columns],
            core_send, core_recv, dy * len(n_out) + j, sibling,
        )

    def y_copy(j):
        columns = pl.ds(*n_out[j])
        return remote(to_y.at[:, columns], from_y.at[:, columns], y_send, y_recv, j, beside)

    def z_copy(j, d):
        columns = pl.ds(*n_out[j])
        return remote(
            to_z.at[pl.ds(d * rows, rows), columns], from_z.at[pl.ds(d * rows, rows), columns],
            z_send, z_recv, j * 3 + d - 1, along[d],
        )

    for d in range(FAR):
        gather_c[0, d].wait_recv()
    loads[0].wait()
    loads[1].wait()
    for at, size in n_ff:
        up_tile(0, at, size)
    for d in range(FAR):
        gather_y[d].wait_recv()
        gather_c[1, d].start()
    loads[2].wait()
    for j, (at, size) in enumerate(n_out):
        down_tile(0, at, size)
        core_copy(0, j).start()

    for d in range(FAR):
        gather_c[1, d].wait_recv()
    for at, size in n_ff:
        up_tile(1, at, size)

    def after_core(j):
        at, size = n_out[j]
        core_copy(1, j).wait_recv()
        to_y[:, at : at + size] = (
            y[2 * quad : 3 * quad, at : at + size].astype(jnp.float32)
            + from_core[quad : 2 * quad, at : at + size].astype(jnp.float32)
        ).astype(jnp.bfloat16)
        y_copy(j).start()

    def after_y(j):
        at, size = n_out[j]
        core_copy(0, j).wait_recv()
        y_copy(j).wait_recv()
        to_z[:, at : at + size] = (
            y[0:quad, at : at + size].astype(jnp.float32)
            + from_core[0:quad, at : at + size].astype(jnp.float32)
            + from_y[:, at : at + size].astype(jnp.float32)
        ).astype(jnp.bfloat16)
        for d in (3, 2, 1):
            z_copy(j, d).start()

    count = len(n_out)
    for j, (at, size) in enumerate(n_out):
        down_tile(1, at, size)
        core_copy(1, j).start()
        if j >= 1:
            after_core(j - 1)
    after_core(count - 1)
    for j in range(count):
        after_y(j)
    for j, (at, size) in enumerate(n_out):
        total = to_z[0:rows, at : at + size].astype(jnp.float32)
        for d in (1, 2, 3):
            z_copy(j, d).wait_recv()
            total += from_z[d * rows : (d + 1) * rows, at : at + size].astype(jnp.float32)
        out_ref[:, at : at + size] = total.astype(jnp.bfloat16)

    for copy in [*gather_z.values(), *gather_y.values(), *gather_c.values()]:
        copy.wait_send()
    for j in range(count):
        core_copy(0, j).wait_send()
        core_copy(1, j).wait_send()
        y_copy(j).wait_send()
        for d in (1, 2, 3):
            z_copy(j, d).wait_send()


def gather_body(hidden_a, routes, gate_w, w_gate, w_up, w_down):
    experts = lax.axis_size(("attn", "expert"))
    rows, width = hidden_a.shape
    ff = w_gate.shape[2]
    wide = -(-width // LANES) * LANES
    quad = FAR * rows
    count = len(tiles_of(width, 512))
    vmem = pl.BlockSpec(memory_space=pltpu.VMEM)
    hbm = pl.BlockSpec(memory_space=pl.ANY)
    dma = pltpu.SemaphoreType.DMA
    tokens = experts * rows
    return pl.pallas_call(
        kernel,
        out_shape=jax.ShapeDtypeStruct((rows, width), jnp.bfloat16),
        in_specs=[vmem, vmem, vmem, hbm, hbm, hbm],
        out_specs=vmem,
        scratch_shapes=[
            pltpu.VMEM((width, ff), jnp.bfloat16),
            pltpu.VMEM((width, ff), jnp.bfloat16),
            pltpu.VMEM((ff, width), jnp.bfloat16),
            pltpu.VMEM((tokens, wide), jnp.bfloat16),
            pltpu.VMEM((tokens // 2, ff), jnp.bfloat16),
            pltpu.VMEM((tokens, width), jnp.bfloat16),
            pltpu.VMEM((tokens // 2, width), jnp.bfloat16),
            pltpu.VMEM((quad, width), jnp.bfloat16),
            pltpu.VMEM((quad, width), jnp.bfloat16),
            pltpu.VMEM((quad, width), jnp.bfloat16),
            pltpu.VMEM((quad, width), jnp.bfloat16),
            dma((3,)),
            dma((15,)),
            dma((15,)),
            dma((2 * count,)),
            dma((2 * count,)),
            dma((count,)),
            dma((count,)),
            dma((3 * count,)),
            dma((3 * count,)),
        ],
        compiler_params=pltpu.CompilerParams(
            collective_id=0, has_side_effects=True, vmem_limit_bytes=56 * 1024 * 1024
        ),
        cost_estimate=pl.CostEstimate(
            flops=6 * tokens * width * ff, bytes_accessed=6 * width * ff, transcendentals=tokens * ff
        ),
    )(hidden_a, routes, gate_w, w_gate, w_up, w_down)


def solution(mesh):
    placed = (
        P(("groups", "attn", "expert"), None),
        P(("groups", "attn", "expert"), None),
        P(("groups", "attn", "expert"), None),
        P(("attn", "expert"), None, None),
        P(("attn", "expert"), None, None),
        P(("attn", "expert"), None, None),
    )
    small = mesh.shape["attn"] == 2 and mesh.shape["expert"] == 2 * FAR
    return jax.shard_map(
        gather_body if small else exchange_body,
        mesh=mesh,
        in_specs=placed,
        out_specs=P(("groups", "attn", "expert"), None),
        check_vma=False,
    )
```

time: 86.1 us -> 48 us (0.56)
  waiting for transfers between devices: 46 us -> 0 us
  Pallas kernels: 0 us -> 43.6 us
  starting transfers between devices: 14.6 us -> 0 us
  matrix products: 12.5 us -> 0 us
  local copies, waits for them, and re-layouts: 9.11 us -> 4.27 us
  other arithmetic: 3.35 us -> 0 us
    all_to_all x3 -> x0, waiting for transfers between devices: 46 us -> none  [the longest x1 21.1 us: body(): lax.all_to_all(produced, ('attn', 'expert'), split_axis=0, concat_axis=0,...]
    pallas_call x0 -> x1, Pallas kernels: none -> 43.6 us  [gather_body(): pl.pallas_call(kernel, out_shape=jax.ShapeDtypeStruct((rows, width), jnp....]
    all_to_all x3 -> x0, starting transfers between devices: 14.6 us -> none  [the longest x1 7.39 us: body(): lax.all_to_all(send_weights, ('attn', 'expert'), split_axis=0, concat_axi...]
    dot_general x2 -> x0, matrix products: 12.5 us -> none  [the longest x1 8.31 us: body(): down = jnp.dot(hidden, down_matrix, preferred_element_type=jnp.float32)]
    gather x4 -> x0, local copies, waits for them, and re-layouts: 4.13 us -> none  [the longest x1 1.87 us: body(): gate_w.reshape(-1)[safe]]
    unnamed x4 -> x3, local copies, waits for them, and re-layouts: 1.58 us -> 4.27 us
    reduce_sum x2 -> x0, other arithmetic: 1.34 us -> none  [the longest x1 1.17 us: body(): jnp.sum(taken.astype(jnp.float32).reshape(tok_dev, top_k, width), axis=1)]
    convert_element_type x2 -> x0, local copies, waits for them, and re-layouts: 1.23 us -> none  [the longest x1 1.15 us: body(): produced = scaled.astype(jnp.bfloat16).reshape(senders, slots, width)]
  transfers between devices with their start and end apart: 3 -> 0, of which waited for: 3 -> 0; matrix products, arithmetic and copies ran while one was open for 3% -> 0% of each run, Pallas kernels for 0% -> 0%
where the time goes in v1:
time: 48 us; the launch traced here: 47.8 us
  Pallas kernels  43.6 us (91%)
  local copies, waits for them, and re-layouts  4.27 us (9%)
    pallas_call x1, Pallas kernels, gather_body(): pl.pallas_call(kernel, out_shape=jax.ShapeDtypeStruct((rows, width), jnp....  43.6 us
    unnamed x3, local copies, waits for them, and re-layouts  4.27 us

profile of v1, /device:TPU:0, one launch (start us, length us, event | category | flops | bytes accessed | tf_op | source)
XLA Modules:
  0.0 47.8 jit_solution(10481199615194665739)
XLA Ops:
  0.0 1.4 %copy.8.gates_ref = bf16[32,4]{1,0:T(8,128)(2,1)} copy(bf16[32,4]{0,1:T(4,128)(2,1)} %param.8) | data formatting | bytes 512 | tf_op args[2]
  1.4 1.4 %copy.7.routes_ref = s32[32,4]{1,0:T(8,128)} copy(s32[32,4]{0,1:T(4,128)} %param.7) | data formatting | bytes 1024 | tf_op args[1]
  2.7 43.6 %shard_map.64 = bf16[32,1440]{1,0:T(8,128)(2,1)} custom-call(bf16[32,1440]{1,0:T(8,128)(2,1)} %hidden_ref.1, s32[32,4]{1,0:T(8,128)} %copy.7.routes_ref, bf16[32,4]{1,0:T(8,128)(2,1)} %copy.8.gates_ref, bf16[1,1440,1440]{2,1,0:T(8,128)(2,1)} %wg_hbm.1, bf16[1,1440,1440]{2,1,0:T(8,128)(2,1)} %wu_hbm.1, bf16[1,1440,1440]{2,1,0:T(8,128)(2,1)} %wd_hbm.1), custom_call_target="tpu_custom_call" | custom-call | flops 6370099200 | bytes 12441600 | tf_op jit(solution)/shard_map/pallas_call | solution.py:246
  46.3 1.5 %copy.10 = bf16[32,1440]{1,0:T(8,128)(2,1)} copy(bf16[32,1440]{1,0:T(8,128)(2,1)} %shard_map.64) | data formatting | bytes 184320

commit v2 on v1

--- a/solution.py
+++ b/solution.py
@@ -57,12 +57,12 @@
 
 
 def kernel(
-    hidden_ref, routes_ref, gates_ref, wg_hbm, wu_hbm, wd_hbm, out_ref,
-    wg, wu, wd, x, h, y, from_core, to_y, from_y, to_z, from_z,
+    hidden_hbm, routes_hbm, gates_hbm, wg_hbm, wu_hbm, wd_hbm, out_ref,
+    tokens, named, gates, wg, wu, wd, x, h, y, from_core, to_y, from_y, to_z, from_z,
     load_sem, ag_send, ag_recv, core_send, core_recv, y_send, y_recv, z_send, z_recv,
 ):
-    rows, top = routes_ref.shape
-    width = hidden_ref.shape[1]
+    top, rows = routes_hbm.shape
+    width = hidden_hbm.shape[1]
     ff = wg_hbm.shape[2]
     quad = FAR * rows
 
@@ -77,11 +77,15 @@
     beside = (group, core, far * 2 + 1 - near)
     along = [(group, core, f * 2 + near) for f in fars]
 
+    inputs = [
+        pltpu.make_async_copy(src, dst, load_sem.at[i])
+        for i, (src, dst) in enumerate(((hidden_hbm, tokens), (routes_hbm, named), (gates_hbm, gates)))
+    ]
     loads = [
-        pltpu.make_async_copy(src.at[0], dst, load_sem.at[i])
+        pltpu.make_async_copy(src.at[0], dst, load_sem.at[3 + i])
         for i, (src, dst) in enumerate(((wg_hbm, wg), (wu_hbm, wu), (wd_hbm, wd)))
     ]
-    for load in loads:
+    for load in inputs:
         load.start()
 
     barrier = pltpu.get_barrier_semaphore()
@@ -89,47 +93,82 @@
     for partner in partners:
         pl.semaphore_signal(barrier, inc=1, device_id=partner, device_id_type=MESH)
 
+    for load in loads:
+        load.start()
+    for load in inputs:
+        load.wait()
+
     start = width // LANES * LANES
     rest = width - start
-    x[0:rows, 0:start] = hidden_ref[:, 0:start]
-    lane = lax.broadcasted_iota(jnp.int32, (rows, LANES), 1)
-    table = jnp.zeros((rows, LANES), jnp.float32)
+    x[0:rows, 0:start] = tokens[:, 0:start]
+    lane = lax.broadcasted_iota(jnp.int32, (LANES, rows), 0)
+    weights = gates[...].astype(jnp.float32)
+    table = jnp.zeros((LANES, rows), jnp.float32)
     for k in range(top):
-        table += jnp.where(
-            lane == routes_ref[:, k : k + 1] + rest, gates_ref[:, k : k + 1].astype(jnp.float32), 0.0
-        )
+        table += jnp.where(lane == named[k : k + 1, :] + rest, weights[k : k + 1, :], 0.0)
     last = jnp.concatenate(
-        [hidden_ref[:, start:].astype(jnp.float32), jnp.zeros((rows, LANES - rest), jnp.float32)], axis=1
-    )
-    x[0:rows, start : start + LANES] = (table + last).astype(jnp.bfloat16)
+        [tokens[:, start:].astype(jnp.float32), jnp.zeros((rows, LANES - rest), jnp.float32)], axis=1
+    )
+    x[0:rows, start : start + LANES] = (table.T + last).astype(jnp.bfloat16)
     pl.semaphore_wait(barrier, len(partners))
 
-    def slot(dy, dc, d):
-        return x.at[pl.ds(((dy * 2 + dc) * FAR + d) * rows, rows)]
-
-    def remote(src, dst, send, recv, i, device):
+    half = rows // 2
+
+    def piece(dy, dc, d, p):
+        return x.at[pl.ds(((dy * 2 + dc) * FAR + d) * rows + p * half, half)]
+
+    def remote(src, dst, send, recv, device):
         return pltpu.make_async_remote_copy(
-            src_ref=src, dst_ref=dst, send_sem=send.at[i], recv_sem=recv.at[i],
+            src_ref=src, dst_ref=dst, send_sem=send, recv_sem=recv,
             device_id=device, device_id_type=MESH,
         )
 
-    gather_z = {d: remote(slot(0, 0, 0), slot(0, 0, d), ag_send, ag_recv, d - 1, along[d]) for d in (1, 2, 3)}
-    gather_y = {d: remote(slot(0, 0, d), slot(1, 0, d), ag_send, ag_recv, 3 + d, beside) for d in range(FAR)}
+    def gather(src, dst, i, device):
+        return remote(src, dst, ag_send.at[i], ag_recv.at[i], device)
+
+    middle = (far + 1) // 2 == 1
+    pieces = range(2)
+    gather_z = {
+        (d, p): gather(piece(0, 0, 0, p), piece(0, 0, d, p), (d - 1) * 2 + p, along[d])
+        for d in (1, 2, 3) for p in pieces
+    }
+    gather_y = {
+        (d, p): gather(piece(0, 0, d, p), piece(1, 0, d, p), 6 + d * 2 + p, beside)
+        for d in range(FAR) for p in pieces
+    }
     gather_c = {
-        (dy, d): remote(slot(dy, 0, d), slot(dy, 1, d), ag_send, ag_recv, 7 + dy * FAR + d, sibling)
-        for dy in range(2) for d in range(FAR)
+        (dy, d, p): gather(piece(dy, 0, d, p), piece(dy, 1, d, p), 14 + (dy * FAR + d) * 2 + p, sibling)
+        for dy in range(2) for d in range(FAR) for p in pieces
     }
-    for d in (3, 2, 1):
-        gather_z[d].start()
-    gather_y[0].start()
-    gather_c[0, 0].start()
-    for d in (1, 2, 3):
-        gather_z[d].wait_recv()
-        gather_y[d].start()
-        gather_c[0, d].start()
+    passed = {
+        p: remote(piece(0, 0, 2, p), piece(0, 0, 3, p), ag_send.at[30 + p], ag_recv.at[4 + p], along[1])
+        for p in pieces
+    }
+    for p in pieces:
+        gather_z[2, p].start()
+        gather_z[1, p].start()
+        gather_y[0, p].start()
+
+    @pl.when(middle)
+    def _():
+        for p in pieces:
+            gather_z[3, p].start()
+
+    for p in pieces:
+        gather_c[0, 0, p].start()
+    for d, p in ((2, 0), (1, 0), (2, 1), (1, 1), (3, 0), (3, 1)):
+        gather_z[d, p].wait_recv()
+        if d == 2:
+
+            @pl.when(middle)
+            def _():
+                passed[p].start()
+
+        gather_y[d, p].start()
+        gather_c[0, d, p].start()
 
     n_ff = tiles_of(ff, 512)
-    n_out = tiles_of(width, 512)
+    n_out = tiles_of(width, 256)
     scale = {}
 
     def up_tile(dy, at, size):
@@ -146,48 +185,63 @@
         down = jnp.dot(h[...], wd[:, at : at + size], preferred_element_type=jnp.float32)
         y[dy * 2 * quad : (dy + 1) * 2 * quad, at : at + size] = (scale[dy] * down).astype(jnp.bfloat16)
 
-    def core_copy(dy, j):
-        at, size = n_out[j]
-        columns = pl.ds(at, size)
+    early = remote(
+        y.at[pl.ds(quad, quad)], from_core.at[pl.ds(0, quad)], core_send.at[0], core_recv.at[0], sibling
+    )
+
+    def core_copy(j):
+        columns = pl.ds(*n_out[j])
         return remote(
-            y.at[pl.ds((dy * 2 + 1) * quad, quad), columns],
-            from_core.at[pl.ds(dy * quad, quad), columns],
-            core_send, core_recv, dy * len(n_out) + j, sibling,
+            y.at[pl.ds(3 * quad, quad), columns],
+            from_core.at[pl.ds(quad, quad), columns],
+            core_send.at[1 + j], core_recv.at[1 + j], sibling,
         )
 
     def y_copy(j):
         columns = pl.ds(*n_out[j])
-        return remote(to_y.at[:, columns], from_y.at[:, columns], y_send, y_recv, j, beside)
+        return remote(to_y.at[:, columns], from_y.at[:, columns], y_send.at[j], y_recv.at[j], beside)
 
     def z_copy(j, d):
         columns = pl.ds(*n_out[j])
+        i = j * 3 + d - 1
         return remote(
             to_z.at[pl.ds(d * rows, rows), columns], from_z.at[pl.ds(d * rows, rows), columns],
-            z_send, z_recv, j * 3 + d - 1, along[d],
+            z_send.at[i], z_recv.at[i], along[d],
         )
 
     for d in range(FAR):
-        gather_c[0, d].wait_recv()
+        for p in pieces:
+            gather_c[0, d, p].wait_recv()
     loads[0].wait()
     loads[1].wait()
     for at, size in n_ff:
         up_tile(0, at, size)
-    for d in range(FAR):
-        gather_y[d].wait_recv()
-        gather_c[1, d].start()
+    queue = [(0, 0), (0, 1), (2, 0), (1, 0), (2, 1), (1, 1), (3, 0), (3, 1)]
+
+    def hand_on(many):
+        for _ in range(many):
+            d, p = queue.pop(0)
+            gather_y[d, p].wait_recv()
+            gather_c[1, d, p].start()
+
+    hand_on(4)
     loads[2].wait()
     for j, (at, size) in enumerate(n_out):
         down_tile(0, at, size)
-        core_copy(0, j).start()
+        if j >= 1 and len(queue) > 0:
+            hand_on(1)
+    hand_on(len(queue))
+    early.start()
 
     for d in range(FAR):
-        gather_c[1, d].wait_recv()
+        for p in pieces:
+            gather_c[1, d, p].wait_recv()
     for at, size in n_ff:
         up_tile(1, at, size)
 
     def after_core(j):
         at, size = n_out[j]
-        core_copy(1, j).wait_recv()
+        core_copy(j).wait_recv()
         to_y[:, at : at + size] = (
             y[2 * quad : 3 * quad, at : at + size].astype(jnp.float32)
             + from_core[quad : 2 * quad, at : at + size].astype(jnp.float32)
@@ -196,7 +250,6 @@
 
     def after_y(j):
         at, size = n_out[j]
-        core_copy(0, j).wait_recv()
         y_copy(j).wait_recv()
         to_z[:, at : at + size] = (
             y[0:quad, at : at + size].astype(jnp.float32)
@@ -209,10 +262,11 @@
     count = len(n_out)
     for j, (at, size) in enumerate(n_out):
         down_tile(1, at, size)
-        core_copy(1, j).start()
+        core_copy(j).start()
         if j >= 1:
             after_core(j - 1)
     after_core(count - 1)
+    early.wait_recv()
     for j in range(count):
         after_y(j)
     for j, (at, size) in enumerate(n_out):
@@ -222,11 +276,21 @@
             total += from_z[d * rows : (d + 1) * rows, at : at + size].astype(jnp.float32)
         out_ref[:, at : at + size] = total.astype(jnp.bfloat16)
 
-    for copy in [*gather_z.values(), *gather_y.values(), *gather_c.values()]:
+    for d in (1, 2):
+        for p in pieces:
+            gather_z[d, p].wait_send()
+
+    @pl.when(middle)
+    def _():
+        for p in pieces:
+            gather_z[3, p].wait_send()
+            passed[p].wait_send()
+
+    for copy in [*gather_y.values(), *gather_c.values()]:
         copy.wait_send()
+    early.wait_send()
     for j in range(count):
-        core_copy(0, j).wait_send()
-        core_copy(1, j).wait_send()
+        core_copy(j).wait_send()
         y_copy(j).wait_send()
         for d in (1, 2, 3):
             z_copy(j, d).wait_send()
@@ -238,7 +302,7 @@
     ff = w_gate.shape[2]
     wide = -(-width // LANES) * LANES
     quad = FAR * rows
-    count = len(tiles_of(width, 512))
+    count = len(tiles_of(width, 256))
     vmem = pl.BlockSpec(memory_space=pltpu.VMEM)
     hbm = pl.BlockSpec(memory_space=pl.ANY)
     dma = pltpu.SemaphoreType.DMA
@@ -246,9 +310,12 @@
     return pl.pallas_call(
         kernel,
         out_shape=jax.ShapeDtypeStruct((rows, width), jnp.bfloat16),
-        in_specs=[vmem, vmem, vmem, hbm, hbm, hbm],
+        in_specs=[hbm] * 6,
         out_specs=vmem,
         scratch_shapes=[
+            pltpu.VMEM((rows, width), jnp.bfloat16),
+            pltpu.VMEM(routes.shape[::-1], jnp.int32),
+            pltpu.VMEM(gate_w.shape[::-1], jnp.bfloat16),
             pltpu.VMEM((width, ff), jnp.bfloat16),
             pltpu.VMEM((width, ff), jnp.bfloat16),
             pltpu.VMEM((ff, width), jnp.bfloat16),
@@ -260,11 +327,11 @@
             pltpu.VMEM((quad, width), jnp.bfloat16),
             pltpu.VMEM((quad, width), jnp.bfloat16),
             pltpu.VMEM((quad, width), jnp.bfloat16),
-            dma((3,)),
-            dma((15,)),
-            dma((15,)),
-            dma((2 * count,)),
-            dma((2 * count,)),
+            dma((6,)),
+            dma((32,)),
+            dma((30,)),
+            dma((1 + count,)),
+            dma((1 + count,)),
             dma((count,)),
             dma((count,)),
             dma((3 * count,)),
@@ -276,7 +343,7 @@
         cost_estimate=pl.CostEstimate(
             flops=6 * tokens * width * ff, bytes_accessed=6 * width * ff, transcendentals=tokens * ff
         ),
-    )(hidden_a, routes, gate_w, w_gate, w_up, w_down)
+    )(hidden_a, routes.T, gate_w.T, w_gate, w_up, w_down)
 
 
 def solution(mesh):

time: 48 us -> 42.9 us (0.89)
  local copies, waits for them, and re-layouts: 4.27 us -> 1.54 us
  Pallas kernels: 43.6 us -> 41.2 us
    unnamed x3 -> x1, local copies, waits for them, and re-layouts: 4.27 us -> 1.54 us
    pallas_call x1, Pallas kernels: 43.6 us -> 41.2 us  [gather_body(): pl.pallas_call(kernel, out_shape=jax.ShapeDtypeStruct((rows, width), jnp....]
where the time goes in v2:
time: 42.9 us; the launch traced here: 42.8 us
  Pallas kernels  41.2 us (96%)
  local copies, waits for them, and re-layouts  1.54 us (4%)
    pallas_call x1, Pallas kernels, gather_body(): pl.pallas_call(kernel, out_shape=jax.ShapeDtypeStruct((rows, width), jnp....  41.2 us
    unnamed x1, local copies, waits for them, and re-layouts  1.54 us

profile of v2, /device:TPU:0, one launch (start us, length us, event | category | flops | bytes accessed | tf_op | source)
XLA Modules:
  0.0 42.8 jit_solution(9632204560050757980)
XLA Ops:
  0.0 41.2 %shard_map.64 = bf16[32,1440]{1,0:T(8,128)(2,1)} custom-call(bf16[32,1440]{1,0:T(8,128)(2,1)} %hidden_hbm.1, s32[4,32]{1,0:T(4,128)} %bitcast.2, bf16[4,32]{1,0:T(4,128)(2,1)} %bitcast.3, bf16[1,1440,1440]{2,1,0:T(8,128)(2,1)} %wg_hbm.1, bf16[1,1440,1440]{2,1,0:T(8,128)(2,1)} %wu_hbm.1, bf16[1,1440,1440]{2,1,0:T(8,128)(2,1)} %wd_hbm.1), custom_call_target="tpu_custom_call" | custom-call | flops 6370099200 | bytes 12441600 | tf_op jit(solution)/shard_map/pallas_call | solution.py:310
  41.3 1.5 %copy.8 = bf16[32,1440]{1,0:T(8,128)(2,1)} copy(bf16[32,1440]{1,0:T(8,128)(2,1)} %shard_map.64) | data formatting | bytes 184320

commit v3 on v2

--- a/solution.py
+++ b/solution.py
@@ -112,7 +112,7 @@
     x[0:rows, start : start + LANES] = (table.T + last).astype(jnp.bfloat16)
     pl.semaphore_wait(barrier, len(partners))
 
-    half = rows // 2
+    half = rows
 
     def piece(dy, dc, d, p):
         return x.at[pl.ds(((dy * 2 + dc) * FAR + d) * rows + p * half, half)]
@@ -127,7 +127,7 @@
         return remote(src, dst, ag_send.at[i], ag_recv.at[i], device)
 
     middle = (far + 1) // 2 == 1
-    pieces = range(2)
+    pieces = range(1)
     gather_z = {
         (d, p): gather(piece(0, 0, 0, p), piece(0, 0, d, p), (d - 1) * 2 + p, along[d])
         for d in (1, 2, 3) for p in pieces
@@ -156,7 +156,7 @@
 
     for p in pieces:
         gather_c[0, 0, p].start()
-    for d, p in ((2, 0), (1, 0), (2, 1), (1, 1), (3, 0), (3, 1)):
+    for d, p in ((1, 0), (2, 0), (3, 0)):
         gather_z[d, p].wait_recv()
         if d == 2:
 
@@ -216,7 +216,7 @@
     loads[1].wait()
     for at, size in n_ff:
         up_tile(0, at, size)
-    queue = [(0, 0), (0, 1), (2, 0), (1, 0), (2, 1), (1, 1), (3, 0), (3, 1)]
+    queue = [(0, 0), (1, 0), (2, 0), (3, 0)]
 
     def hand_on(many):
         for _ in range(many):
@@ -224,7 +224,7 @@
             gather_y[d, p].wait_recv()
             gather_c[1, d, p].start()
 
-    hand_on(4)
+    hand_on(2)
     loads[2].wait()
     for j, (at, size) in enumerate(n_out):
         down_tile(0, at, size)

time: 42.9 us -> 41.9 us (0.977)
  Pallas kernels: 41.2 us -> 40.2 us
    pallas_call x1, Pallas kernels: 41.2 us -> 40.2 us  [gather_body(): pl.pallas_call(kernel, out_shape=jax.ShapeDtypeStruct((rows, width), jnp....]
where the time goes in v3:
time: 41.9 us; the launch traced here: 41.7 us
  Pallas kernels  40.2 us (96%)
  local copies, waits for them, and re-layouts  1.54 us (4%)
    pallas_call x1, Pallas kernels, gather_body(): pl.pallas_call(kernel, out_shape=jax.ShapeDtypeStruct((rows, width), jnp....  40.2 us
    unnamed x1, local copies, waits for them, and re-layouts  1.54 us

profile of v3, /device:TPU:0, one launch (start us, length us, event | category | flops | bytes accessed | tf_op | source)
XLA Modules:
  0.0 41.7 jit_solution(10100498776556781573)
XLA Ops:
  0.0 40.2 %shard_map.64 = bf16[32,1440]{1,0:T(8,128)(2,1)} custom-call(bf16[32,1440]{1,0:T(8,128)(2,1)} %hidden_hbm.1, s32[4,32]{1,0:T(4,128)} %bitcast.2, bf16[4,32]{1,0:T(4,128)(2,1)} %bitcast.3, bf16[1,1440,1440]{2,1,0:T(8,128)(2,1)} %wg_hbm.1, bf16[1,1440,1440]{2,1,0:T(8,128)(2,1)} %wu_hbm.1, bf16[1,1440,1440]{2,1,0:T(8,128)(2,1)} %wd_hbm.1), custom_call_target="tpu_custom_call" | custom-call | flops 6370099200 | bytes 12441600 | tf_op jit(solution)/shard_map/pallas_call | solution.py:310
  40.2 1.5 %copy.8 = bf16[32,1440]{1,0:T(8,128)(2,1)} copy(bf16[32,1440]{1,0:T(8,128)(2,1)} %shard_map.64) | data formatting | bytes 184320
